TPU v7x, 256 devices: a whole 4x4x8 slice. The times are simulated.
256 devices in a mesh: row: 16 (over z_lo, y, core), col: 16 (over x, z_hi).
Axes of the slice: x: 4, y: 4, z: 8 (z_hi: 4, z_lo: 2; z = z_hi * 2 + z_lo), core: 2. Of those that a mesh axis runs over, the one named last changes fastest.
Arguments:
- block_input: bfloat16 [2048, 8192], P('col', 'row'), may hold values from -6 to 6
- out_grad: bfloat16 [2048, 8192], P('col', 'row'), may hold values from -6 to 6
- gate_pre: bfloat16 [2048, 14336], P('row', 'col'), may hold values from -8 to 8
- up_pre: bfloat16 [2048, 14336], P('row', 'col'), may hold values from -6 to 6
- gate_weight: bfloat16 [8192, 14336], P('row', 'col'), may hold values from -0.0625 to 0.0625
- up_weight: bfloat16 [8192, 14336], P('row', 'col'), may hold values from -0.0625 to 0.0625
- down_weight: bfloat16 [8192, 14336], P('row', 'col'), may hold values from -0.046875 to 0.046875
Outputs:
- input_grad: bfloat16 [2048, 8192], P('col', 'row')
- grad_gate: float32 [8192, 14336], P('row', 'col')
- grad_up: float32 [8192, 14336], P('row', 'col')
- grad_down: float32 [8192, 14336], P('row', 'col')
All inputs are finite; a program needn't handle non-finite values.
Results may differ from a plain program's by a relative error of at most 0.0049.
Values may be sent and summed in bfloat16 or wider, within the bound.
A program may use at most 128 MiB of HBM per device.

v0:
```python
import jax
import jax.numpy as jnp
from jax import lax
from jax.sharding import PartitionSpec as P


def local_grads(hidden_grad, gate_pre, up_pre):
    gate_f = gate_pre.astype(jnp.float32)
    up_f = up_pre.astype(jnp.float32)
    sig = jax.nn.sigmoid(gate_f)
    hidden = (gate_f * sig * up_f).astype(jnp.bfloat16)
    up_delta = (hidden_grad * gate_f * sig).astype(jnp.bfloat16)
    gate_delta = (hidden_grad * up_f * sig * (1.0 + gate_f * (1.0 - sig))).astype(jnp.bfloat16)
    return (hidden, gate_delta, up_delta)


def body(block_input, out_grad, gate_pre, up_pre, gate_weight, up_weight, down_weight):
    grad_full, input_full = (
        lax.all_gather(out_grad, "col", axis=0, tiled=True),
        lax.all_gather(block_input, "col", axis=0, tiled=True),
    )
    hidden_part = lax.psum_scatter(
        jnp.dot(grad_full, down_weight, preferred_element_type=jnp.float32),
        "row",
        scatter_dimension=0,
        tiled=True,
    )
    hidden_mine, gate_mine, up_mine = local_grads(hidden_part, gate_pre, up_pre)
    hidden, gate_delta, up_delta = (
        lax.all_gather(hidden_mine, "row", axis=0, tiled=True),
        lax.all_gather(gate_mine, "row", axis=0, tiled=True),
        lax.all_gather(up_mine, "row", axis=0, tiled=True),
    )
    contract = (((0,), (0,)), ((), ()))
    grad_down = lax.dot_general(grad_full, hidden, contract, preferred_element_type=jnp.float32)
    grad_gate = lax.dot_general(
        input_full, gate_delta, contract, preferred_element_type=jnp.float32
    )
    grad_up = lax.dot_general(input_full, up_delta, contract, preferred_element_type=jnp.float32)
    inner = (((1,), (1,)), ((), ()))
    total = lax.dot_general(gate_delta, gate_weight, inner, preferred_element_type=jnp.float32)
    input_grad = lax.psum_scatter(
        total + lax.dot_general(up_delta, up_weight, inner, preferred_element_type=jnp.float32),
        "col",
        scatter_dimension=0,
        tiled=True,
    )
    return (input_grad.astype(jnp.bfloat16), grad_gate, grad_up, grad_down)


def solution(mesh):
    return jax.shard_map(
        body,
        mesh=mesh,
        in_specs=(
            P("col", "row"),
            P("col", "row"),
            P("row", "col"),
            P("row", "col"),
            P("row", "col"),
            P("row", "col"),
            P("row", "col"),
        ),
        out_specs=(P("col", "row"), P("row", "col"), P("row", "col"), P("row", "col")),
        check_vma=False,
    )
```

profile of v0, /device:TPU:32, one launch (start us, length us, event | category | flops | bytes accessed | tf_op | source)
XLA Modules:
  0.0 441.9 jit_solution(3552637911680624528)
XLA Ops:
  7.2 0.0 all-gather.6.cloned.1.call-start
  7.2 0.7 all-gather.6.cloned.1.call-update
  7.9 0.0 reduce-scatter.3.cloned.1.call-start
  8.0 63.2 %all-gather.6.cloned.1.call-done = bf16[2048,512]{1,0:T(8,128)(2,1)} async-done(((bf16[128,512]{1,0:T(8,128)(2,1)}), bf16[2048,512]{1,0:T(8,128)(2,1)}) %all-gather.6.cloned.1.call-update) | async-done | bytes 2097168 | tf_op jit(solution)/shard_map/all_gather | solution.py:19
  71.2 6.9 %fusion.10 = f32[2048,896]{1,0:T(8,128)} fusion(bf16[2048,512]{1,0:T(8,128)(2,1)} %all-gather.6.cloned.1.call-done, bf16[512,896]{1,0:T(8,128)(2,1)S(1)} %copy-done), kind=kOutput, calls=%fused_computation.20 | convolution fusion | flops 1879048192 | bytes 10354688 | tf_op jit(solution)/shard_map/dot_general | solution.py:23
  78.1 0.0 reduce-scatter.3.cloned.1.call-update
  78.1 0.0 all-gather.8.cloned.1.call-start
  78.1 73.7 %reduce-scatter.3.cloned.1.call-done = f32[128,896]{1,0:T(8,128)} async-done(((f32[2048,896]{1,0:T(8,128)}), f32[128,896]{1,0:T(8,128)}) %reduce-scatter.3.cloned.1.call-update) | async-done | bytes 458768 | tf_op jit(solution)/shard_map/reduce_scatter | solution.py:22
  151.9 2.1 fusion.9
  154.0 0.0 all-gather.8.cloned.1.call-update
  154.0 0.0 all-gather.10.cloned.1.call-start
  154.0 0.5 all-gather.10.cloned.1.call-update
  154.6 0.0 all-gather.12.cloned.1.call-start
  154.6 0.5 all-gather.12.cloned.1.call-update
  155.1 0.0 all-gather.14.cloned.1.call-start
  155.2 0.5 all-gather.14.cloned.1.call-update
  155.7 0.0 reduce-scatter.5.cloned.1.call-start
  155.8 36.7 %all-gather.8.cloned.1.call-done = bf16[2048,896]{1,0:T(8,128)(2,1)} async-done(((bf16[128,896]{1,0:T(8,128)(2,1)}), bf16[2048,896]{1,0:T(8,128)(2,1)}) %all-gather.8.cloned.1.call-update) | async-done | bytes 3670032 | tf_op jit(solution)/shard_map/all_gather | solution.py:31
  192.5 6.4 %fusion.11 = f32[2048,512]{1,0:T(8,128)} fusion(bf16[2048,896]{1,0:T(8,128)(2,1)} %all-gather.8.cloned.1.call-done, bf16[512,896]{1,0:T(8,128)(2,1)S(1)} %copy-done.4), kind=kOutput, calls=%fused_computation.21 | convolution fusion | flops 1879048192 | bytes 8781824 | tf_op jit(solution)/shard_map/dot_general | solution.py:41
  198.9 35.3 %all-gather.10.cloned.1.call-done = bf16[2048,896]{1,0:T(8,128)(2,1)} async-done(((bf16[128,896]{1,0:T(8,128)(2,1)}), bf16[2048,896]{1,0:T(8,128)(2,1)}) %all-gather.10.cloned.1.call-update) | async-done | bytes 3670032 | tf_op jit(solution)/shard_map/all_gather | solution.py:32
  234.2 7.6 %convolution_add_fusion = f32[2048,512]{1,0:T(8,128)} fusion(f32[2048,512]{1,0:T(8,128)} %fusion.11, bf16[2048,896]{1,0:T(8,128)(2,1)} %all-gather.10.cloned.1.call-done, bf16[512,896]{1,0:T(8,128)(2,1)S(1)} %copy-done.5), kind=kOutput, calls=%fused_computation | convolution fusion | flops 1880096768 | bytes 12976128 | tf_op jit(solution)/shard_map/dot_general | solution.py:43
  241.8 0.0 reduce-scatter.5.cloned.1.call-update
  241.8 53.1 %all-gather.12.cloned.1.call-done = bf16[2048,512]{1,0:T(8,128)(2,1)} async-done(((bf16[128,512]{1,0:T(8,128)(2,1)}), bf16[2048,512]{1,0:T(8,128)(2,1)}) %all-gather.12.cloned.1.call-update) | async-done | bytes 2097168 | tf_op jit(solution)/shard_map/all_gather | solution.py:20
  294.9 6.0 %convolution_bitcast_fusion.2 = f32[512,896]{0,1:T(8,128)} fusion(bf16[2048,896]{1,0:T(8,128)(2,1)} %all-gather.8.cloned.1.call-done, bf16[2048,512]{1,0:T(8,128)(2,1)} %all-gather.12.cloned.1.call-done), kind=kOutput, calls=%fused_computation.3 | convolution fusion | flops 1879048192 | bytes 7602176 | tf_op jit(solution)/shard_map/dot_general | solution.py:36
  301.0 2.9 copy.11
  303.8 5.4 %convolution_bitcast_fusion.1 = f32[512,896]{0,1:T(8,128)} fusion(bf16[2048,896]{1,0:T(8,128)(2,1)} %all-gather.10.cloned.1.call-done, bf16[2048,512]{1,0:T(8,128)(2,1)S(1)} %copy-done.1), kind=kOutput, calls=%fused_computation.2 | convolution fusion | flops 1879048192 | bytes 7602176 | tf_op jit(solution)/shard_map/dot_general | solution.py:39
  309.2 2.7 copy.12
  311.9 23.1 %all-gather.14.cloned.1.call-done = bf16[2048,896]{1,0:T(8,128)(2,1)} async-done(((bf16[128,896]{1,0:T(8,128)(2,1)}), bf16[2048,896]{1,0:T(8,128)(2,1)}) %all-gather.14.cloned.1.call-update) | async-done | bytes 3670032 | tf_op jit(solution)/shard_map/all_gather | solution.py:30
  335.0 4.8 %convolution_bitcast_fusion = f32[512,896]{0,1:T(8,128)S(1)} fusion(bf16[2048,896]{1,0:T(8,128)(2,1)} %all-gather.14.cloned.1.call-done, bf16[2048,512]{1,0:T(8,128)(2,1)} %all-gather.6.cloned.1.call-done), kind=kOutput, calls=%fused_computation.1 | convolution fusion | flops 1879048192 | bytes 7602176 | tf_op jit(solution)/shard_map/dot_general | solution.py:35
  339.8 1.7 copy.13
  341.4 92.0 %reduce-scatter.5.cloned.1.call-done = f32[128,512]{1,0:T(8,128)} async-done(((f32[2048,512]{1,0:T(8,128)}), f32[128,512]{1,0:T(8,128)}) %reduce-scatter.5.cloned.1.call-update) | async-done | bytes 262160 | tf_op jit(solution)/shard_map/reduce_scatter | solution.py:42
  433.4 1.6 convert_element_type.22
  (12 shorter events, 0.0 us)
Async XLA Ops:
  7.2 64.0 %copy-start = (bf16[512,896]{1,0:T(8,128)(2,1)S(1)}, bf16[512,896]{1,0:T(8,128)(2,1)}, u32[]{:S(2)}) copy-start(bf16[512,896]{1,0:T(8,128)(2,1)} %param.13) | copy-start | bytes 2752516
  7.2 64.0 %all-gather.6.cloned.1.call-start = ((), (), s32[]{:S(2)}) async-start(), calls=%async_computation.2 | async-start | bytes 2228224 | tf_op jit(solution)/shard_map/all_gather | solution.py:19
  7.9 143.9 %reduce-scatter.3.cloned.1.call-start = ((), (), s32[]{:S(2)}) async-start(), calls=%async_computation.3 | async-start | bytes 7798784 | tf_op jit(solution)/shard_map/reduce_scatter | solution.py:22
  78.1 73.8 %copy-start.2 = (bf16[128,896]{1,0:T(8,128)(2,1)S(1)}, bf16[128,896]{1,0:T(8,128)(2,1)}, u32[]{:S(2)}) copy-start(bf16[128,896]{1,0:T(8,128)(2,1)} %param.9) | copy-start | bytes 688132
  78.1 73.8 %copy-start.3 = (bf16[128,896]{1,0:T(8,128)(2,1)S(1)}, bf16[128,896]{1,0:T(8,128)(2,1)}, u32[]{:S(2)}) copy-start(bf16[128,896]{1,0:T(8,128)(2,1)} %param.10) | copy-start | bytes 688132
  78.1 114.5 %copy-start.4 = (bf16[512,896]{1,0:T(8,128)(2,1)S(1)}, bf16[512,896]{1,0:T(8,128)(2,1)}, u32[]{:S(2)}) copy-start(bf16[512,896]{1,0:T(8,128)(2,1)} %param.11) | copy-start | bytes 2752516
  78.1 114.4 %all-gather.8.cloned.1.call-start = ((), (), s32[]{:S(2)}) async-start(), calls=%async_computation.4 | async-start | bytes 3899392 | tf_op jit(solution)/shard_map/all_gather | solution.py:31
  154.0 80.2 %all-gather.10.cloned.1.call-start = ((), (), s32[]{:S(2)}) async-start(), calls=%async_computation.5 | async-start | bytes 3899392 | tf_op jit(solution)/shard_map/all_gather | solution.py:32
  154.6 140.4 %all-gather.12.cloned.1.call-start = ((), (), s32[]{:S(2)}) async-start(), calls=%async_computation.7 | async-start | bytes 2228224 | tf_op jit(solution)/shard_map/all_gather | solution.py:20
  155.1 179.8 %all-gather.14.cloned.1.call-start = ((), (), s32[]{:S(2)}) async-start(), calls=%async_computation.8 | async-start | bytes 3899392 | tf_op jit(solution)/shard_map/all_gather | solution.py:30
  155.7 78.5 %copy-start.5 = (bf16[512,896]{1,0:T(8,128)(2,1)S(1)}, bf16[512,896]{1,0:T(8,128)(2,1)}, u32[]{:S(2)}) copy-start(bf16[512,896]{1,0:T(8,128)(2,1)} %param.12) | copy-start | bytes 2752516
  155.7 277.7 %reduce-scatter.5.cloned.1.call-start = ((), (), s32[]{:S(2)}) async-start(), calls=%async_computation.6 | async-start | bytes 4456448 | tf_op jit(solution)/shard_map/reduce_scatter | solution.py:42
  301.0 2.9 copy-start.1
Sparse Core Ops, SparseCore 0:
  10.4 60.6 all-gather.5
  78.2 73.6 reduce-scatter.2
  154.3 38.1 all-gather.7
  194.8 39.3 all-gather.9
  236.5 58.4 all-gather.11
  296.6 38.2 all-gather.13
  338.6 94.8 reduce-scatter.4
where the time goes:
time: 444 us; the launch traced here: 442 us
  waiting for transfers between devices  379 us (85%)
  matrix products  37 us (8%)
  between operations  14.2 us (3%)
  local copies, waits for them, and re-layouts  7.31 us (2%)
    reduce_scatter x1, waiting for transfers between devices, body(): lax.psum_scatter(total + lax.dot_general(up_delta, up_weight, inner, pref...  92 us
    reduce_scatter x1, waiting for transfers between devices, body(): lax.psum_scatter(jnp.dot(grad_full, down_weight, preferred_element_type=j...  73.7 us
    all_gather x1, waiting for transfers between devices, body(): lax.all_gather(out_grad, 'col', axis=0, tiled=True)  63.2 us
    all_gather x1, waiting for transfers between devices, body(): lax.all_gather(block_input, 'col', axis=0, tiled=True)  53.1 us
    all_gather x1, waiting for transfers between devices, body(): lax.all_gather(gate_mine, 'row', axis=0, tiled=True)  36.7 us
    all_gather x1, waiting for transfers between devices, body(): lax.all_gather(up_mine, 'row', axis=0, tiled=True)  35.3 us
    all_gather x1, waiting for transfers between devices, body(): lax.all_gather(hidden_mine, 'row', axis=0, tiled=True)  23.1 us
  transfers between devices with their start and end apart: 7, of which 7 were waited for; matrix products, arithmetic and copies ran while one was open for 8% of the time, Pallas kernels for 0%

commit v1 on v0

v1 whole, which is shorter than its diff:
```python
import jax
import jax.numpy as jnp
from jax import lax
from jax.experimental import pallas as pl
from jax.experimental.pallas import tpu as pltpu
from jax.sharding import PartitionSpec as P

MESH = pl.DeviceIdType.MESH
BF = jnp.bfloat16
F32 = jnp.float32
T, D, F = 128, 512, 896
Q = 32


def dot(a, b):
    return jnp.dot(a, b, preferred_element_type=F32)


def dot_nt(a, b):
    return lax.dot_general(a, b, (((1,), (1,)), ((), ())), preferred_element_type=F32)


def dot_tn(a, b):
    return lax.dot_general(a, b, (((0,), (0,)), ((), ())), preferred_element_type=F32)


def kernel(
    x_in, g_in, gate_in, up_in, wg_in, wu_in, wd_in,
    ig_out, gg_out, gu_out, gd_out,
    GF, GS, XF, GA, UP, HP, HR, HO, HZS, HZR, HG, HID, DG, DU,
    IPO, IPS, IPR, IZS, IZR, WD, WDS, WG, WU, OUT, IGO,
    lsem, osem, bs, br, xs, xr, rs, rr, ss, sr,
):
    row = lax.axis_index("row")
    col = lax.axis_index("col")
    zl, y, k = row // 8, (row // 2) % 4, row % 2
    x, zh = col // 4, col % 4

    def at(dzl=0, dy=0, dk=0, dx=0, dzh=0):
        r = ((zl + dzl) % 2) * 8 + ((y + dy) % 4) * 2 + (k + dk) % 2
        c = ((x + dx) % 4) * 4 + (zh + dzh) % 4
        return {"row": r, "col": c}

    started = []

    def send(src, dst, send_sem, recv_sem, dev):
        cp = pltpu.make_async_remote_copy(
            src_ref=src, dst_ref=dst, send_sem=send_sem, recv_sem=recv_sem, device_id=dev, device_id_type=MESH
        )
        cp.start()
        started.append(cp)

    def arrived(dst, recv_sem):
        pltpu.make_async_copy(dst, dst, recv_sem).wait()

    peers = [at(dk=1), at(dzl=1)]
    for d in (1, 2, 3):
        peers += [at(dy=d), at(dx=d), at(dzh=d)]
    barrier = pltpu.get_barrier_semaphore()
    for p in peers:
        pl.semaphore_signal(barrier, inc=1, device_id=p, device_id_type=MESH)
    pl.semaphore_wait(barrier, len(peers))

    def blk(xx, zz):
        xx, zz = (xx + 8) % 4, (zz + 8) % 4
        return zz % 2, 2 * xx + zz // 2

    myp, myh = blk(x, zh)
    mine = 4 * zl + y
    other = 4 * (1 - zl) + y

    for e in (1, 3, 2):
        send(g_in, GF.at[myp, myh], bs.at[0, e, 0], br.at[0, e, 0], at(dzh=e))
    for d in (1, 3, 2):
        send(g_in, GF.at[myp, myh], bs.at[0, 0, d], br.at[0, 0, d], at(dx=d))
    loads = []
    for i, (src, dst) in enumerate(
        [
            (g_in, GF.at[myp, myh]), (wd_in, WD), (gate_in, GA.at[mine]), (up_in, UP.at[mine]),
            (x_in, XF.at[myp, myh]), (wg_in, WG), (wu_in, WU),
        ]
    ):
        cp = pltpu.make_async_copy(src, dst, lsem.at[i])
        cp.start()
        loads.append(cp)
    send(wd_in, WDS, ss.at[0], sr.at[0], at(dk=1))

    for d in (1, 3, 2):
        send(gate_in, GA.at[mine], rs.at[0, d], rr.at[0, d], at(dy=d))
        send(up_in, UP.at[mine], rs.at[1, d], rr.at[1, d], at(dy=d))
    send(gate_in, GA.at[mine], rs.at[0, 0], rr.at[0, 0], at(dzl=1))
    send(up_in, UP.at[mine], rs.at[1, 0], rr.at[1, 0], at(dzl=1))

    def forward_x(buf, i):
        for e in (1, 3, 2):
            p, h = blk(x, zh - e)
            arrived(buf.at[p, h], br.at[i, e, 0])
            for d in (1, 3, 2):
                send(buf.at[p, h], buf.at[p, h], bs.at[i, e, d], br.at[i, e, d], at(dx=d))

    def wait_x(buf, i, d):
        for e in range(4):
            p, h = blk(x - d, zh - e)
            arrived(buf.at[p, h], br.at[i, e, d])

    forward_x(GF, 0)

    for e in (1, 3, 2):
        send(x_in, XF.at[myp, myh], bs.at[1, e, 0], br.at[1, e, 0], at(dzh=e))

    arrived(GA.at[other], rr.at[0, 0])
    for d in (1, 3, 2):
        send(GA.at[other], GA.at[other], rs.at[0, 4 + d], rr.at[0, 4 + d], at(dy=d))
    for d in (1, 3, 2):
        h = 4 * zl + (y + 4 - d) % 4
        arrived(UP.at[h], rr.at[1, d])
        send(UP.at[h], UP.at[h], rs.at[1, 4 + d], rr.at[1, 4 + d], at(dzl=1))

    loads[0].wait()
    loads[1].wait()

    order = (1, 3, 2, 0)

    def base(n):
        return 2 * ((x + 4 - order[n]) % 4)

    def to_sibling(n):
        if order[n]:
            wait_x(GF, 0, order[n])
        b = base(n)
        send(GF.at[1 - k, pl.ds(b, 2)], GS.at[pl.ds(b, 2)], ss.at[1 + n], sr.at[1 + n], at(dk=1))

    def stage_a(n):
        b = base(n)
        arrived(GS.at[pl.ds(b, 2)], sr.at[1 + n])
        if n == 0:
            arrived(WDS, sr.at[0])
        part = dot(GF[k, pl.ds(b, 2)].reshape(2 * T, D), WD[...])
        part = part + dot(GS[pl.ds(b, 2)].reshape(2 * T, D), WDS[...])
        part = part.astype(BF).reshape(2, 4, Q, F)
        for yy in range(4):
            HP[n, yy] = part[:, yy]
        for d in (1, 3, 2):
            send(HP.at[n, (y + d) % 4], HR.at[n, d - 1], xs.at[n, d], xr.at[n, d], at(dy=d))

    def stage_b(n):
        for d in (1, 3, 2):
            arrived(HR.at[n, d - 1], xr.at[n, d])

        def total(z):
            t = HP[n, y, z].astype(F32)
            for d in range(3):
                t = t + HR[n, d, z].astype(F32)
            return t

        HZS[n] = total(1 - zl)
        send(HZS.at[n], HZR.at[n], xs.at[n, 0], xr.at[n, 0], at(dzl=1))
        HO[n] = total(zl)

    def stage_c(n):
        b = base(n)
        arrived(HZR.at[n], xr.at[n, 0])
        HG[b + zl, y] = (HO[n] + HZR[n]).astype(BF)
        own = HG.at[b + zl, y]
        send(own, own, xs.at[n, 4], xr.at[n, 4], at(dzl=1))
        for d in (1, 3, 2):
            send(own, own, xs.at[n, 4 + d], xr.at[n, 4 + d], at(dy=d))

    def stage_d(n):
        b = base(n)
        theirs = HG.at[b + 1 - zl, y]
        arrived(theirs, xr.at[n, 4])
        for d in (1, 3, 2):
            send(theirs, theirs, xs.at[n, 8 + d], xr.at[n, 8 + d], at(dy=d))

    def stage_e(n):
        b = base(n)
        for d in (1, 3, 2):
            yy = (y + 4 - d) % 4
            arrived(HG.at[b + zl, yy], xr.at[n, 4 + d])
            arrived(HG.at[b + 1 - zl, yy], xr.at[n, 8 + d])
        if n == 0:
            loads[2].wait()
            loads[3].wait()
            for d in (1, 3, 2):
                yy = (y + 4 - d) % 4
                arrived(GA.at[4 * zl + yy], rr.at[0, d])
                arrived(GA.at[4 * (1 - zl) + yy], rr.at[0, 4 + d])
                arrived(UP.at[4 * (1 - zl) + yy], rr.at[1, 4 + d])
            arrived(UP.at[other], rr.at[1, 0])

        def tile(t, _):
            i, j = b + t // 8, t % 8
            rows = pl.ds(pl.multiple_of(j * 16, 16), 16)
            hg = HG[i, j // 2, pl.ds(pl.multiple_of((j % 2) * 16, 16), 16), :].astype(F32)
            ga = GA[i, rows, :].astype(F32)
            up = UP[i, rows, :].astype(F32)
            sig = jax.nn.sigmoid(ga)
            gs = ga * sig
            HID[k, i, rows, :] = (gs * up).astype(BF)
            DU[k, i, rows, :] = (hg * gs).astype(BF)
            DG[k, i, rows, :] = (hg * up * sig * (1.0 + ga * (1.0 - sig))).astype(BF)
            return 0

        lax.fori_loop(0, 16, tile, 0)
        for j, buf in enumerate((DG, DU, HID)):
            part = buf.at[k, pl.ds(b, 2)]
            send(part, part, ss.at[5 + 3 * n + j], sr.at[5 + 3 * n + j], at(dk=1))

    def stage_f(n):
        b = base(n)
        if n == 0:
            loads[5].wait()
            loads[6].wait()
        for p in range(2):
            if p == 0:
                for j, buf in enumerate((DG, DU)):
                    arrived(buf.at[1 - k, pl.ds(b, 2)], sr.at[5 + 3 * n + j])
            part = dot_nt(DG[p, pl.ds(b, 2)].reshape(2 * T, F), WG[...])
            part = part + dot_nt(DU[p, pl.ds(b, 2)].reshape(2 * T, F), WU[...])
            part = part.reshape(2, T, D)
            if order[n]:
                IPS[n, p] = part.astype(BF)
            else:
                IPO[p] = part
        if order[n]:
            send(IPS.at[n], IPR.at[n], xs.at[n, 12], xr.at[n, 12], at(dx=4 - order[n]))

    to_sibling(3)
    to_sibling(0)
    stage_a(0)
    for d in (1, 3, 2):
        send(x_in, XF.at[myp, myh], bs.at[1, 0, d], br.at[1, 0, d], at(dx=d))
    to_sibling(1)
    stage_a(1)
    stage_b(0)
    to_sibling(2)
    stage_a(2)
    stage_b(1)
    stage_c(0)
    forward_x(XF, 1)
    stage_a(3)
    stage_b(2)
    stage_c(1)
    stage_d(0)
    stage_b(3)
    stage_c(2)
    stage_d(1)
    stage_e(0)
    stage_c(3)
    stage_d(2)
    stage_f(0)
    stage_e(1)
    stage_d(3)
    stage_f(1)
    stage_e(2)
    stage_f(2)
    stage_e(3)
    stage_f(3)

    for n in range(3):
        arrived(IPR.at[n], xr.at[n, 12])
    for p in range(2):
        for i in range(2):
            t = IPO[p, i]
            for n in range(3):
                t = t + IPR[n, p, i].astype(F32)
            IZS[p, i] = t.astype(BF)
            IPO[p, i] = t
    for e in (2, 1, 3):
        zz = (zh + e) % 4
        send(IZS.at[zz % 2, zz // 2], IZR.at[e - 1], rs.at[2, e], rr.at[2, e], at(dzh=e))

    for n in range(4):
        b = base(n)
        arrived(HID.at[1 - k, pl.ds(b, 2)], sr.at[5 + 3 * n + 2])
    outs = []

    def weight_grad(i, lhs, rhs, out):
        a = lhs[...].reshape(16 * T, D)

        def cols(j, _):
            c = pl.ds(pl.multiple_of(j * 128, 128), 128)
            OUT[i, :, c] = dot_tn(a, rhs[:, :, :, c].reshape(16 * T, 128))
            return 0

        lax.fori_loop(0, F // 128, cols, 0)
        cp = pltpu.make_async_copy(OUT.at[i], out, osem.at[i])
        cp.start()
        outs.append(cp)

    weight_grad(0, GF, HID, gd_out)
    loads[4].wait()
    for d in (1, 3, 2):
        wait_x(XF, 1, d)
    weight_grad(1, XF, DG, gg_out)
    weight_grad(2, XF, DU, gu_out)

    t = IPO[myp, zh // 2]
    for e in (1, 2, 3):
        arrived(IZR.at[e - 1], rr.at[2, e])
        t = t + IZR[e - 1].astype(F32)
    IGO[...] = t.astype(BF)
    cp = pltpu.make_async_copy(IGO, ig_out, osem.at[3])
    cp.start()
    outs.append(cp)
    for cp in outs:
        cp.wait()
    for cp in started:
        cp.wait_send()


def body(*args):
    any_spec = pl.BlockSpec(memory_space=pl.ANY)
    dma = pltpu.SemaphoreType.DMA
    return pl.pallas_call(
        kernel,
        out_shape=[
            jax.ShapeDtypeStruct((T, D), BF),
            jax.ShapeDtypeStruct((D, F), F32),
            jax.ShapeDtypeStruct((D, F), F32),
            jax.ShapeDtypeStruct((D, F), F32),
        ],
        in_specs=[any_spec] * 7,
        out_specs=[any_spec] * 4,
        scratch_shapes=[
            pltpu.VMEM((2, 8, T, D), BF),
            pltpu.VMEM((8, T, D), BF),
            pltpu.VMEM((2, 8, T, D), BF),
            pltpu.VMEM((8, T, F), BF),
            pltpu.VMEM((8, T, F), BF),
            pltpu.VMEM((4, 4, 2, Q, F), BF),
            pltpu.VMEM((4, 3, 2, Q, F), BF),
            pltpu.VMEM((4, Q, F), F32),
            pltpu.VMEM((4, Q, F), F32),
            pltpu.VMEM((4, Q, F), F32),
            pltpu.VMEM((8, 4, Q, F), BF),
            pltpu.VMEM((2, 8, T, F), BF),
            pltpu.VMEM((2, 8, T, F), BF),
            pltpu.VMEM((2, 8, T, F), BF),
            pltpu.VMEM((2, 2, T, D), F32),
            pltpu.VMEM((3, 2, 2, T, D), BF),
            pltpu.VMEM((3, 2, 2, T, D), BF),
            pltpu.VMEM((2, 2, T, D), BF),
            pltpu.VMEM((3, T, D), BF),
            pltpu.VMEM((D, F), BF),
            pltpu.VMEM((D, F), BF),
            pltpu.VMEM((D, F), BF),
            pltpu.VMEM((D, F), BF),
            pltpu.VMEM((3, D, F), F32),
            pltpu.VMEM((T, D), BF),
            dma((7,)),
            dma((4,)),
            dma((2, 4, 4)),
            dma((2, 4, 4)),
            dma((4, 13)),
            dma((4, 13)),
            dma((3, 8)),
            dma((3, 8)),
            dma((17,)),
            dma((17,)),
        ],
        compiler_params=pltpu.CompilerParams(
            collective_id=0, has_side_effects=True, vmem_limit_bytes=56 * 1024 * 1024
        ),
        cost_estimate=pl.CostEstimate(flops=12 * 2048 * D * F, bytes_accessed=10 << 20, transcendentals=0),
        name="swiglu_backward",
    )(*args)


def solution(mesh):
    return jax.shard_map(
        body,
        mesh=mesh,
        in_specs=(
            P("col", "row"),
            P("col", "row"),
            P("row", "col"),
            P("row", "col"),
            P("row", "col"),
            P("row", "col"),
            P("row", "col"),
        ),
        out_specs=(P("col", "row"), P("row", "col"), P("row", "col"), P("row", "col")),
        check_vma=False,
    )
```

time: 444 us -> 142 us (0.32)
  waiting for transfers between devices: 379 us -> 0 us
  Pallas kernels: 0 us -> 131 us
  matrix products: 37 us -> 0 us
  between operations: 14.2 us -> 0.64 us
    all_gather x5 -> x0, waiting for transfers between devices: 211 us -> none  [the longest x1 63.2 us: body(): lax.all_gather(out_grad, 'col', axis=0, tiled=True)]
    reduce_scatter x2 -> x0, waiting for transfers between devices: 166 us -> none  [the longest x1 92 us: body(): lax.psum_scatter(total + lax.dot_general(up_delta, up_weight, inner, pref...]
    pallas_call x0 -> x1, Pallas kernels: none -> 131 us  [body(): pl.pallas_call(kernel, out_shape=[jax.ShapeDtypeStruct((T, D), BF), jax.S...]
    dot_general x6 -> x0, matrix products: 37 us -> none  [the longest x1 7.62 us: body(): lax.dot_general(up_delta, up_weight, inner, preferred_element_type=jnp.fl...]
  transfers between devices with their start and end apart: 7 -> 0, of which waited for: 7 -> 0; matrix products, arithmetic and copies ran while one was open for 8% -> 0% of each run, Pallas kernels for 0% -> 0%
where the time goes in v1:
time: 142 us; the launch traced here: 139 us
  Pallas kernels  131 us (92%)
  local copies, waits for them, and re-layouts  7.94 us (6%)
    pallas_call x1, Pallas kernels, body(): pl.pallas_call(kernel, out_shape=[jax.ShapeDtypeStruct((T, D), BF), jax.S...  131 us
    unnamed x8, local copies, waits for them, and re-layouts  7.94 us

profile of v1, /device:TPU:32, one launch (start us, length us, event | category | flops | bytes accessed | tf_op | source)
XLA Modules:
  0.0 139.4 jit_solution(1050749059749777407)
XLA Ops:
  0.6 130.8 %swiglu_backward.1 = (bf16[128,512]{1,0:T(8,128)(2,1)}, f32[512,896]{1,0:T(8,128)}, f32[512,896]{1,0:T(8,128)}, f32[512,896]{1,0:T(8,128)}) custom-call(bf16[128,512]{1,0:T(8,128)(2,1)} %x_in.1, bf16[128,512]{1,0:T(8,128)(2,1)} %g_in.1, bf16[128,896]{1,0:T(8,128)(2,1)} %gate_in.1, bf16[128,896]{1,0:T(8,128)(2,1)} %up_in.1, bf16[512,896]{1,0:T(8,128)(2,1)} %wg_in.1, ...), custom_call_target="tpu_custom_call" | custom-call | flops 11274289152 | bytes 10485760 | tf_op jit(solution)/shard_map/swiglu_backward/pallas_call | solution.py:316
  131.4 1.6 %copy.15 = bf16[128,512]{1,0:T(8,128)(2,1)} copy(bf16[128,512]{1,0:T(8,128)(2,1)} %get-tuple-element.8) | data formatting | bytes 262144
  133.0 0.0 copy-start.1
  133.0 3.0 %copy.16 = f32[512,896]{1,0:T(8,128)} copy(f32[512,896]{1,0:T(8,128)} %get-tuple-element.9) | data formatting | bytes 3670016
  136.0 0.0 copy-done.1
  136.0 0.0 copy-start
  136.0 1.2 copy.17
  137.2 0.9 copy-done
  138.1 1.2 copy.18
Async XLA Ops:
  133.0 3.0 %copy-start.1 = (f32[512,896]{1,0:T(8,128)S(1)}, f32[512,896]{1,0:T(8,128)}, u32[]{:S(2)}) copy-start(f32[512,896]{1,0:T(8,128)} %get-tuple-element.10) | copy-start | bytes 5505028
  136.0 2.2 %copy-start = (f32[512,896]{1,0:T(8,128)S(1)}, f32[512,896]{1,0:T(8,128)}, u32[]{:S(2)}) copy-start(f32[512,896]{1,0:T(8,128)} %get-tuple-element.11) | copy-start | bytes 5505028

commit v2 on v1

v2 whole, which is shorter than its diff:
```python
import jax
import jax.numpy as jnp
from jax import lax
from jax.experimental import pallas as pl
from jax.experimental.pallas import tpu as pltpu
from jax.sharding import PartitionSpec as P

MESH = pl.DeviceIdType.MESH
BF = jnp.bfloat16
F32 = jnp.float32
T, D, F = 128, 512, 896
Q = 32
ZSUM = (0, 1, 1, 0)
ZGATHER = (1, 0, 1, 0)


def dot(a, b):
    return jnp.dot(a, b, preferred_element_type=F32)


def dot_nt(a, b):
    return lax.dot_general(a, b, (((1,), (1,)), ((), ())), preferred_element_type=F32)


def dot_tn(a, b):
    return lax.dot_general(a, b, (((0,), (0,)), ((), ())), preferred_element_type=F32)


def kernel(
    x_in, g_in, gate_in, up_in, wg_in, wu_in, wd_in,
    ig_out, gg_out, gu_out, gd_out,
    GF, GS, XF, GA, UP, FU, FG, HP, HF, HR, HZS, HZR, HG, HID, DG, DU,
    IPO, IPS, IPR, IZ2, IXS, IXR, IZS, IZR, WD, WDS, WG, WU, OUT, IGO,
    lsem, osem, bs, br, xs, xr, rs, rr, ss, sr,
):
    row = lax.axis_index("row")
    col = lax.axis_index("col")
    zl, y, k = row // 8, (row // 2) % 4, row % 2
    x, zh = col // 4, col % 4

    def at(dzl=0, dy=0, dk=0, dx=0, dzh=0):
        r = ((zl + dzl) % 2) * 8 + ((y + dy) % 4) * 2 + (k + dk) % 2
        c = ((x + dx) % 4) * 4 + (zh + dzh) % 4
        return {"row": r, "col": c}

    started = []

    def send(src, dst, send_sem, recv_sem, dev):
        cp = pltpu.make_async_remote_copy(
            src_ref=src, dst_ref=dst, send_sem=send_sem, recv_sem=recv_sem, device_id=dev, device_id_type=MESH
        )
        cp.start()
        started.append(cp)

    def arrived(dst, recv_sem):
        pltpu.make_async_copy(dst, dst, recv_sem).wait()

    def blk(xx, zz):
        xx, zz = (xx + 8) % 4, (zz + 8) % 4
        return zz % 2, 2 * xx + zz // 2

    myp, myh = blk(x, zh)
    mine = 4 * zl + y
    other = 4 * (1 - zl) + y

    loads = []
    for i, (src, dst) in enumerate(
        [
            (g_in, GF.at[myp, myh]), (wd_in, WD), (gate_in, GA.at[mine]), (up_in, UP.at[mine]),
            (x_in, XF.at[myp, myh]), (wg_in, WG), (wu_in, WU),
        ]
    ):
        cp = pltpu.make_async_copy(src, dst, lsem.at[i])
        cp.start()
        loads.append(cp)

    peers = [at(dk=1), at(dzl=1)]
    for d in (1, 2, 3):
        peers += [at(dy=d), at(dx=d), at(dzh=d)]
    barrier = pltpu.get_barrier_semaphore()
    for p in peers:
        pl.semaphore_signal(barrier, inc=1, device_id=p, device_id_type=MESH)
    pl.semaphore_wait(barrier, len(peers))

    for e in (1, 3):
        send(g_in, GF.at[myp, myh], bs.at[0, e, 0], br.at[0, e, 0], at(dzh=e))
    for d in (1, 3):
        send(g_in, GF.at[myp, myh], bs.at[0, 0, d], br.at[0, 0, d], at(dx=d))
    for i, src, buf in ((0, gate_in, GA), (1, up_in, UP)):
        for d in (1, 3):
            send(src, buf.at[mine], rs.at[i, d], rr.at[i, d], at(dy=d))
    send(wd_in, WDS, ss.at[0], sr.at[0], at(dk=1))

    HALF = (pl.ds(0, T // 2), pl.ds(T // 2, T // 2))

    def forward_z(buf, i, e):
        p, h = blk(x, zh - e)
        if e == 2:
            for j in range(2):
                arrived(buf.at[p, h, HALF[j]], br.at[i, 2, 5 * j])
        else:
            arrived(buf.at[p, h], br.at[i, e, 0])
            half = buf.at[p, h, HALF[e // 2]]
            send(half, half, bs.at[i, 2, 5 * (e // 2)], br.at[i, 2, 5 * (e // 2)], at(dzh=e))
        for d in (1, 3):
            send(buf.at[p, h], buf.at[p, h], bs.at[i, e, d], br.at[i, e, d], at(dx=d))

    def forward_x(buf, i, e):
        for j, d in enumerate((1, 3)):
            p, h = blk(x - d, zh - e)
            arrived(buf.at[p, h], br.at[i, e, d])
            half = buf.at[p, h, HALF[j]]
            send(half, half, bs.at[i, e, 2 + 2 * j], br.at[i, e, 2 + 2 * j], at(dx=d))

    def wait_x(buf, i, d):
        if d == 2:
            for e in range(4):
                p, h = blk(x - 2, zh - e)
                for j in range(2):
                    arrived(buf.at[p, h, HALF[j]], br.at[i, e, 2 + 2 * j])

    def forward_y(i, buf, z, o):
        for j, d in enumerate((1, 3)):
            h = 4 * z + (y + 4 - d) % 4
            arrived(buf.at[h], rr.at[i, o + d])
            half = buf.at[h, HALF[j]]
            send(half, half, rs.at[i, o + 2 + 2 * j], rr.at[i, o + 2 + 2 * j], at(dy=d))

    def wait_y(i, buf, z, o):
        for j in range(2):
            arrived(buf.at[4 * z + (y + 2) % 4, HALF[j]], rr.at[i, o + 2 + 2 * j])

    def forward_zl(i, buf):
        arrived(buf.at[other], rr.at[i, 0])
        for d in (1, 3):
            send(buf.at[other], buf.at[other], rs.at[i, 5 + d], rr.at[i, 5 + d], at(dy=d))

    order = (1, 3, 2, 0)

    def base(n):
        return 2 * ((x + 4 - order[n]) % 4)

    def to_sibling(n):
        if order[n]:
            wait_x(GF, 0, order[n])
        else:
            loads[0].wait()
        b = base(n)
        send(GF.at[1 - k, pl.ds(b, 2)], GS.at[pl.ds(b, 2)], ss.at[1 + n], sr.at[1 + n], at(dk=1))

    def stage_a(n):
        b = base(n)
        arrived(GS.at[pl.ds(b, 2)], sr.at[1 + n])
        if n == 3:
            loads[1].wait()
            arrived(WDS, sr.at[0])
        part = dot(GF[k, pl.ds(b, 2)].reshape(2 * T, D), WD[...])
        part = (part + dot(GS[pl.ds(b, 2)].reshape(2 * T, D), WDS[...])).reshape(2, 4, Q, F)
        if ZSUM[n]:
            part = part.reshape(8, Q, F)
            HF[n] = part
            HP[n] = part.astype(BF)
            send(HP.at[n, pl.ds(4 * (1 - zl), 4)], HR.at[n, pl.ds(0, 4)], xs.at[n, 0], xr.at[n, 0], at(dzl=1))
        else:
            for yy in range(4):
                HF[n, 2 * yy : 2 * yy + 2] = part[:, yy]
                HP[n, 2 * yy : 2 * yy + 2] = part[:, yy].astype(BF)
            for d in (1, 3, 2):
                to = 2 * ((y + d) % 4)
                send(HP.at[n, pl.ds(to, 2)], HR.at[n, pl.ds(2 * d - 2, 2)], xs.at[n, d], xr.at[n, d], at(dy=d))

    def stage_b(n):
        if ZSUM[n]:
            arrived(HR.at[n, pl.ds(0, 4)], xr.at[n, 0])
            for yy in range(4):
                t = HF[n, 4 * zl + yy] + HR[n, yy].astype(F32)
                HF[n, 4 * zl + yy] = t
                HP[n, 4 * zl + yy] = t.astype(BF)
            for d in (1, 3, 2):
                to = 4 * zl + (y + d) % 4
                send(HP.at[n, to], HR.at[n, 3 + d], xs.at[n, d], xr.at[n, d], at(dy=d))
        else:
            for d in (1, 3, 2):
                arrived(HR.at[n, pl.ds(2 * d - 2, 2)], xr.at[n, d])

            def total(z):
                t = HF[n, 2 * y + z]
                for d in (1, 2, 3):
                    t = t + HR[n, 2 * d - 2 + z].astype(F32)
                return t

            HZS[n] = total(1 - zl)
            send(HZS.at[n], HZR.at[n], xs.at[n, 0], xr.at[n, 0], at(dzl=1))
            HF[n, 2 * y + zl] = total(zl)

    def stage_c(n):
        b = base(n)
        if ZSUM[n]:
            for d in (1, 3, 2):
                arrived(HR.at[n, 3 + d], xr.at[n, d])
            t = HF[n, 4 * zl + y]
            for d in (1, 2, 3):
                t = t + HR[n, 3 + d].astype(F32)
        else:
            arrived(HZR.at[n], xr.at[n, 0])
            t = HF[n, 2 * y + zl] + HZR[n]
        HG[b + zl, y] = t.astype(BF)
        own = HG.at[b + zl, y]
        send(own, own, xs.at[n, 8], xr.at[n, 8], at(dzl=1))
        for d in (1, 3, 2):
            send(own, own, xs.at[n, 8 + d], xr.at[n, 8 + d], at(dy=d))

    def stage_d(n):
        b = base(n)
        if ZGATHER[n]:
            theirs = HG.at[b + 1 - zl, y]
            arrived(theirs, xr.at[n, 8])
            for d in (1, 3, 2):
                send(theirs, theirs, xs.at[n, 11 + d], xr.at[n, 11 + d], at(dy=d))
        else:
            for d in (1, 3, 2):
                theirs = HG.at[b + zl, (y + 4 - d) % 4]
                arrived(theirs, xr.at[n, 8 + d])
                send(theirs, theirs, xs.at[n, 11 + d], xr.at[n, 11 + d], at(dzl=1))

    def stage_e(n):
        b = base(n)
        for d in (1, 3, 2):
            yy = (y + 4 - d) % 4
            if ZGATHER[n]:
                arrived(HG.at[b + zl, yy], xr.at[n, 8 + d])
            arrived(HG.at[b + 1 - zl, yy], xr.at[n, 11 + d])
        if not ZGATHER[n]:
            arrived(HG.at[b + 1 - zl, y], xr.at[n, 8])
        def tile(t, _):
            i, j = b + t // 8, t % 8
            rows = pl.ds(pl.multiple_of(j * 16, 16), 16)
            hg = HG[i, j // 2, pl.ds(pl.multiple_of((j % 2) * 16, 16), 16), :].astype(F32)
            DU[k, i, rows, :] = (hg * FU[i, rows, :]).astype(BF)
            DG[k, i, rows, :] = (hg * FG[i, rows, :]).astype(BF)
            return 0

        lax.fori_loop(0, 16, tile, 0)
        for j, buf in enumerate((DG, DU)):
            part = buf.at[k, pl.ds(b, 2)]
            send(part, part, ss.at[5 + 3 * n + j], sr.at[5 + 3 * n + j], at(dk=1))

    def stage_p(n):
        b = base(n)

        def tile(t, _):
            i, j = b + t // 8, t % 8
            rows = pl.ds(pl.multiple_of(j * 16, 16), 16)
            ga = GA[i, rows, :].astype(F32)
            up = UP[i, rows, :].astype(F32)
            sig = jax.nn.sigmoid(ga)
            gs = ga * sig
            HID[k, i, rows, :] = (gs * up).astype(BF)
            FU[i, rows, :] = gs
            FG[i, rows, :] = up * sig * (1.0 + ga * (1.0 - sig))
            return 0

        lax.fori_loop(0, 16, tile, 0)
        part = HID.at[k, pl.ds(b, 2)]
        send(part, part, ss.at[7 + 3 * n], sr.at[7 + 3 * n], at(dk=1))

    def stage_f(n):
        b = base(n)
        if n == 0:
            loads[5].wait()
            loads[6].wait()
        for j, buf in enumerate((DG, DU)):
            arrived(buf.at[1 - k, pl.ds(b, 2)], sr.at[5 + 3 * n + j])
        for q in (1, 0):
            p = (zh + q) % 2
            part = dot_nt(DG[p, pl.ds(b, 2)].reshape(2 * T, F), WG[...])
            part = part + dot_nt(DU[p, pl.ds(b, 2)].reshape(2 * T, F), WU[...])
            part = part.reshape(2, T, D)
            if n == 2:
                IPS[n, q] = part.astype(BF)
                for e in (1, 3) if q else (2,):
                    send(IPS.at[n, q, (zh + e) % 4 // 2], IZ2.at[e - 1], rs.at[2, 4 + e], rr.at[2, 4 + e], at(dzh=e))
                if q == 0:
                    IPO[2] = part
            elif order[n]:
                IPS[n, q] = part.astype(BF)
                send(IPS.at[n, q], IPR.at[n, q], xs.at[n, 15 + q], xr.at[n, 15 + q], at(dx=4 - order[n]))
            else:
                IPO[q] = part

    def sum_z2():
        t = IPO[2, zh // 2]
        for e in (1, 3, 2):
            arrived(IZ2.at[e - 1], rr.at[2, 4 + e])
            t = t + IZ2[e - 1].astype(F32)
        IXS[...] = t.astype(BF)
        send(IXS, IXR, rs.at[2, 8], rr.at[2, 8], at(dx=2))

    def sum_x(q):
        for n in range(2):
            arrived(IPR.at[n, q], xr.at[n, 15 + q])
        for i in range(2):
            t = IPO[q, i]
            for n in range(2):
                t = t + IPR[n, q, i].astype(F32)
            IZS[q, i] = t.astype(BF)
            IPO[q, i] = t
        for e in (1, 3) if q else (2,):
            send(IZS.at[q, (zh + e) % 4 // 2], IZR.at[e - 1], rs.at[2, e], rr.at[2, e], at(dzh=e))

    def send_zl():
        for i, src, buf in ((0, gate_in, GA), (1, up_in, UP)):
            send(src, buf.at[mine], rs.at[i, 0], rr.at[i, 0], at(dzl=1))

    def input_z():
        for e in (1, 3):
            send(x_in, XF.at[myp, myh], bs.at[1, e, 0], br.at[1, e, 0], at(dzh=e))

    def input_x():
        for d in (1, 3):
            send(x_in, XF.at[myp, myh], bs.at[1, 0, d], br.at[1, 0, d], at(dx=d))

    def gates_here():
        loads[2].wait()
        loads[3].wait()
        for i, buf in ((0, GA), (1, UP)):
            wait_y(i, buf, zl, 0)
            wait_y(i, buf, 1 - zl, 5)

    outs = []

    def weight_grad(i, lhs, rhs, out):
        if i == 0:
            for n in range(4):
                arrived(HID.at[1 - k, pl.ds(base(n), 2)], sr.at[7 + 3 * n])
        if i == 1:
            loads[4].wait()
            wait_x(XF, 1, 2)
        OUT[i] = dot_tn(lhs[...].reshape(16 * T, D), rhs[...].reshape(16 * T, F))
        cp = pltpu.make_async_copy(OUT.at[i], out, osem.at[i])
        cp.start()
        outs.append(cp)

    forward_x(GF, 0, 0)
    forward_z(GF, 0, 1)
    forward_z(GF, 0, 3)
    input_x()
    forward_y(0, GA, zl, 0)
    forward_y(1, UP, zl, 0)
    forward_z(GF, 0, 2)
    send_zl()
    to_sibling(3)
    forward_x(GF, 0, 1)
    forward_x(GF, 0, 3)
    stage_a(3)
    input_z()
    forward_x(GF, 0, 2)
    to_sibling(0)
    to_sibling(1)
    stage_a(0)
    stage_a(1)
    forward_zl(0, GA)
    forward_zl(1, UP)
    to_sibling(2)
    stage_a(2)
    stage_b(0)
    forward_x(XF, 1, 0)
    forward_z(XF, 1, 1)
    forward_z(XF, 1, 3)
    stage_b(3)
    stage_b(1)
    stage_c(0)
    forward_z(XF, 1, 2)
    stage_b(2)
    stage_c(1)
    forward_y(0, GA, 1 - zl, 5)
    forward_y(1, UP, 1 - zl, 5)
    stage_d(0)
    stage_c(2)
    forward_x(XF, 1, 1)
    forward_x(XF, 1, 3)
    forward_x(XF, 1, 2)
    stage_d(1)
    stage_c(3)
    stage_d(2)
    gates_here()
    stage_p(0)
    stage_e(0)
    stage_p(1)
    stage_p(2)
    stage_f(0)
    stage_e(1)
    stage_d(3)
    stage_p(3)
    stage_f(1)
    stage_e(2)
    weight_grad(0, GF, HID, gd_out)
    stage_f(2)
    stage_e(3)
    stage_f(3)
    sum_z2()
    sum_x(1)
    sum_x(0)
    weight_grad(1, XF, DG, gg_out)
    weight_grad(2, XF, DU, gu_out)

    t = IPO[0, zh // 2]
    for e in (1, 2, 3):
        arrived(IZR.at[e - 1], rr.at[2, e])
        t = t + IZR[e - 1].astype(F32)
    arrived(IXR, rr.at[2, 8])
    t = t + IXR[...].astype(F32)
    IGO[...] = t.astype(BF)
    cp = pltpu.make_async_copy(IGO, ig_out, osem.at[3])
    cp.start()
    outs.append(cp)
    for cp in outs:
        cp.wait()
    for cp in started:
        cp.wait_send()


def grads(*args):
    any_spec = pl.BlockSpec(memory_space=pl.ANY)
    dma = pltpu.SemaphoreType.DMA
    return pl.pallas_call(
        kernel,
        out_shape=[
            jax.ShapeDtypeStruct((T, D), BF),
            jax.ShapeDtypeStruct((D, F), F32),
            jax.ShapeDtypeStruct((D, F), F32),
            jax.ShapeDtypeStruct((D, F), F32),
        ],
        in_specs=[any_spec] * 7,
        out_specs=[any_spec] * 4,
        scratch_shapes=[
            pltpu.VMEM((2, 8, T, D), BF),
            pltpu.VMEM((8, T, D), BF),
            pltpu.VMEM((2, 8, T, D), BF),
            pltpu.VMEM((8, T, F), BF),
            pltpu.VMEM((8, T, F), BF),
            pltpu.VMEM((8, T, F), F32),
            pltpu.VMEM((8, T, F), F32),
            pltpu.VMEM((4, 8, Q, F), BF),
            pltpu.VMEM((4, 8, Q, F), F32),
            pltpu.VMEM((4, 7, Q, F), BF),
            pltpu.VMEM((4, Q, F), F32),
            pltpu.VMEM((4, Q, F), F32),
            pltpu.VMEM((8, 4, Q, F), BF),
            pltpu.VMEM((2, 8, T, F), BF),
            pltpu.VMEM((2, 8, T, F), BF),
            pltpu.VMEM((2, 8, T, F), BF),
            pltpu.VMEM((3, 2, T, D), F32),
            pltpu.VMEM((3, 2, 2, T, D), BF),
            pltpu.VMEM((2, 2, 2, T, D), BF),
            pltpu.VMEM((3, T, D), BF),
            pltpu.VMEM((T, D), BF),
            pltpu.VMEM((T, D), BF),
            pltpu.VMEM((2, 2, T, D), BF),
            pltpu.VMEM((3, T, D), BF),
            pltpu.VMEM((D, F), BF),
            pltpu.VMEM((D, F), BF),
            pltpu.VMEM((D, F), BF),
            pltpu.VMEM((D, F), BF),
            pltpu.VMEM((3, D, F), F32),
            pltpu.VMEM((T, D), BF),
            dma((7,)),
            dma((4,)),
            dma((2, 4, 6)),
            dma((2, 4, 6)),
            dma((4, 17)),
            dma((4, 17)),
            dma((3, 10)),
            dma((3, 10)),
            dma((17,)),
            dma((17,)),
        ],
        compiler_params=pltpu.CompilerParams(
            collective_id=0, has_side_effects=True, vmem_limit_bytes=60 * 1024 * 1024
        ),
        cost_estimate=pl.CostEstimate(flops=12 * 2048 * D * F, bytes_accessed=10 << 20, transcendentals=0),
        name="swiglu_backward",
    )(*args)


def hand_over(*refs):
    for src, dst in zip(refs[:4], refs[4:]):
        dst[...] = src[...]


def body(*args):
    outs = grads(*args)
    specs = [pl.BlockSpec((o.shape[0] // 4, o.shape[1]), lambda i: (i, 0)) for o in outs]
    return pl.pallas_call(
        hand_over,
        grid=(4,),
        out_shape=[jax.ShapeDtypeStruct(o.shape, o.dtype) for o in outs],
        in_specs=specs,
        out_specs=specs,
        name="hand_over",
    )(*outs)


def solution(mesh):
    return jax.shard_map(
        body,
        mesh=mesh,
        in_specs=(
            P("col", "row"),
            P("col", "row"),
            P("row", "col"),
            P("row", "col"),
            P("row", "col"),
            P("row", "col"),
            P("row", "col"),
        ),
        out_specs=(P("col", "row"), P("row", "col"), P("row", "col"), P("row", "col")),
        check_vma=False,
    )
```

time: 142 us -> 123 us (0.87); the launches traced: 139 us -> 123 us
  Pallas kernels: 131 us -> 122 us
  local copies, waits for them, and re-layouts: 7.94 us -> 0 us
    pallas_call x1 -> x2, Pallas kernels: 131 us -> 122 us  [the longest x1 116 us: grads(): pl.pallas_call(kernel, out_shape=[jax.ShapeDtypeStruct((T, D), BF), jax.S...]
    unnamed x8 -> x0, local copies, waits for them, and re-layouts: 7.94 us -> none
where the time goes in v2:
time: 123 us
  Pallas kernels  122 us (99%)
    pallas_call x1, Pallas kernels, grads(): pl.pallas_call(kernel, out_shape=[jax.ShapeDtypeStruct((T, D), BF), jax.S...  116 us
    pallas_call x1, Pallas kernels, body(): pl.pallas_call(hand_over, grid=(4,), out_shape=[jax.ShapeDtypeStruct(o.sh...  5.48 us

profile of v2, /device:TPU:32, one launch (start us, length us, event | category | flops | bytes accessed | tf_op | source)
XLA Modules:
  0.0 122.6 jit_solution(3679619640652223047)
XLA Ops:
  0.6 116.4 %swiglu_backward.1 = (bf16[128,512]{1,0:T(8,128)(2,1)}, f32[512,896]{1,0:T(8,128)}, f32[512,896]{1,0:T(8,128)}, f32[512,896]{1,0:T(8,128)}) custom-call(bf16[128,512]{1,0:T(8,128)(2,1)} %x_in.1, bf16[128,512]{1,0:T(8,128)(2,1)} %g_in.1, bf16[128,896]{1,0:T(8,128)(2,1)} %gate_in.1, bf16[128,896]{1,0:T(8,128)(2,1)} %up_in.1, bf16[512,896]{1,0:T(8,128)(2,1)} %wg_in.1, ...), custom_call_target="tpu_custom_call" | custom-call | flops 11274289152 | bytes 10485760 | tf_op jit(solution)/shard_map/swiglu_backward/pallas_call | solution.py:426
  117.1 5.5 %hand_over.1 = (bf16[128,512]{1,0:T(8,128)(2,1)}, f32[512,896]{1,0:T(8,128)}, f32[512,896]{1,0:T(8,128)}, f32[512,896]{1,0:T(8,128)}) custom-call(bf16[128,512]{1,0:T(8,128)(2,1)} %get-tuple-element.8.refs_0_, f32[512,896]{1,0:T(8,128)} %get-tuple-element.9.refs_1_, f32[512,896]{1,0:T(8,128)} %get-tuple-element.10.refs_2_, f32[512,896]{1,0:T(8,128)} %get-tuple-element.11.refs_3_), custom_call_target="tpu_custom_call" | custom-call | tf_op jit(solution)/shard_map/hand_over/pallas_call | solution.py:494

commit v3 on v2

--- a/solution.py
+++ b/solution.py
@@ -160,7 +160,12 @@
             part = part.reshape(8, Q, F)
             HF[n] = part
             HP[n] = part.astype(BF)
-            send(HP.at[n, pl.ds(4 * (1 - zl), 4)], HR.at[n, pl.ds(0, 4)], xs.at[n, 0], xr.at[n, 0], at(dzl=1))
+            if ZSUM[n] == 2:
+                for j in (4, 1, 3, 5, 7, 2, 6):
+                    to = (zl + j // 4) % 2 * 4 + (y + j) % 4
+                    send(HP.at[n, to], HR.at[n, j - 1], xs.at[n, j], xr.at[n, j], at(dzl=j // 4, dy=j % 4))
+            else:
+                send(HP.at[n, pl.ds(4 * (1 - zl), 4)], HR.at[n, pl.ds(0, 4)], xs.at[n, 0], xr.at[n, 0], at(dzl=1))
         else:
             for yy in range(4):
                 HF[n, 2 * yy : 2 * yy + 2] = part[:, yy]
@@ -170,6 +175,8 @@
                 send(HP.at[n, pl.ds(to, 2)], HR.at[n, pl.ds(2 * d - 2, 2)], xs.at[n, d], xr.at[n, d], at(dy=d))
 
     def stage_b(n):
+        if ZSUM[n] == 2:
+            return
         if ZSUM[n]:
             arrived(HR.at[n, pl.ds(0, 4)], xr.at[n, 0])
             for yy in range(4):
@@ -189,13 +196,18 @@
                     t = t + HR[n, 2 * d - 2 + z].astype(F32)
                 return t
 
-            HZS[n] = total(1 - zl)
+            HZS[n] = total(1 - zl).astype(BF)
             send(HZS.at[n], HZR.at[n], xs.at[n, 0], xr.at[n, 0], at(dzl=1))
             HF[n, 2 * y + zl] = total(zl)
 
     def stage_c(n):
         b = base(n)
-        if ZSUM[n]:
+        if ZSUM[n] == 2:
+            t = HF[n, 4 * zl + y]
+            for j in (4, 1, 3, 5, 7, 2, 6):
+                arrived(HR.at[n, j - 1], xr.at[n, j])
+                t = t + HR[n, j - 1].astype(F32)
+        elif ZSUM[n]:
             for d in (1, 3, 2):
                 arrived(HR.at[n, 3 + d], xr.at[n, d])
             t = HF[n, 4 * zl + y]
@@ -203,15 +215,20 @@
                 t = t + HR[n, 3 + d].astype(F32)
         else:
             arrived(HZR.at[n], xr.at[n, 0])
-            t = HF[n, 2 * y + zl] + HZR[n]
+            t = HF[n, 2 * y + zl] + HZR[n].astype(F32)
         HG[b + zl, y] = t.astype(BF)
         own = HG.at[b + zl, y]
         send(own, own, xs.at[n, 8], xr.at[n, 8], at(dzl=1))
         for d in (1, 3, 2):
             send(own, own, xs.at[n, 8 + d], xr.at[n, 8 + d], at(dy=d))
+        if ZGATHER[n] == 2:
+            for d in (1, 3, 2):
+                send(own, own, xs.at[n, 11 + d], xr.at[n, 11 + d], at(dzl=1, dy=d))
 
     def stage_d(n):
         b = base(n)
+        if ZGATHER[n] == 2:
+            return
         if ZGATHER[n]:
             theirs = HG.at[b + 1 - zl, y]
             arrived(theirs, xr.at[n, 8])
@@ -230,7 +247,7 @@
             if ZGATHER[n]:
                 arrived(HG.at[b + zl, yy], xr.at[n, 8 + d])
             arrived(HG.at[b + 1 - zl, yy], xr.at[n, 11 + d])
-        if not ZGATHER[n]:
+        if ZGATHER[n] != 1:
             arrived(HG.at[b + 1 - zl, y], xr.at[n, 8])
         def tile(t, _):
             i, j = b + t // 8, t % 8
@@ -344,7 +361,6 @@
     forward_x(GF, 0, 0)
     forward_z(GF, 0, 1)
     forward_z(GF, 0, 3)
-    input_x()
     forward_y(0, GA, zl, 0)
     forward_y(1, UP, zl, 0)
     forward_z(GF, 0, 2)
@@ -353,6 +369,7 @@
     forward_x(GF, 0, 1)
     forward_x(GF, 0, 3)
     stage_a(3)
+    input_x()
     input_z()
     forward_x(GF, 0, 2)
     to_sibling(0)
@@ -365,42 +382,42 @@
     stage_a(2)
     stage_b(0)
     forward_x(XF, 1, 0)
+    stage_b(1)
+    stage_c(0)
     forward_z(XF, 1, 1)
     forward_z(XF, 1, 3)
-    stage_b(3)
-    stage_b(1)
-    stage_c(0)
-    forward_z(XF, 1, 2)
     stage_b(2)
-    stage_c(1)
     forward_y(0, GA, 1 - zl, 5)
     forward_y(1, UP, 1 - zl, 5)
+    stage_c(1)
     stage_d(0)
+    forward_z(XF, 1, 2)
     stage_c(2)
-    forward_x(XF, 1, 1)
-    forward_x(XF, 1, 3)
-    forward_x(XF, 1, 2)
     stage_d(1)
-    stage_c(3)
-    stage_d(2)
+    stage_b(3)
     gates_here()
     stage_p(0)
     stage_e(0)
     stage_p(1)
+    stage_d(2)
+    stage_f(0)
+    forward_x(XF, 1, 1)
+    forward_x(XF, 1, 3)
+    stage_c(3)
+    stage_e(1)
     stage_p(2)
-    stage_f(0)
-    stage_e(1)
+    stage_f(1)
+    forward_x(XF, 1, 2)
+    stage_e(2)
     stage_d(3)
+    stage_f(2)
     stage_p(3)
-    stage_f(1)
-    stage_e(2)
-    weight_grad(0, GF, HID, gd_out)
-    stage_f(2)
     stage_e(3)
     stage_f(3)
     sum_z2()
     sum_x(1)
     sum_x(0)
+    weight_grad(0, GF, HID, gd_out)
     weight_grad(1, XF, DG, gg_out)
     weight_grad(2, XF, DU, gu_out)
 
@@ -444,8 +461,8 @@
             pltpu.VMEM((4, 8, Q, F), BF),
             pltpu.VMEM((4, 8, Q, F), F32),
             pltpu.VMEM((4, 7, Q, F), BF),
-            pltpu.VMEM((4, Q, F), F32),
-            pltpu.VMEM((4, Q, F), F32),
+            pltpu.VMEM((4, Q, F), BF),
+            pltpu.VMEM((4, Q, F), BF),
             pltpu.VMEM((8, 4, Q, F), BF),
             pltpu.VMEM((2, 8, T, F), BF),
             pltpu.VMEM((2, 8, T, F), BF),
@@ -490,10 +507,10 @@
 
 def body(*args):
     outs = grads(*args)
-    specs = [pl.BlockSpec((o.shape[0] // 4, o.shape[1]), lambda i: (i, 0)) for o in outs]
+    specs = [pl.BlockSpec((o.shape[0] // 2, o.shape[1]), lambda i: (i, 0)) for o in outs]
     return pl.pallas_call(
         hand_over,
-        grid=(4,),
+        grid=(2,),
         out_shape=[jax.ShapeDtypeStruct(o.shape, o.dtype) for o in outs],
         in_specs=specs,
         out_specs=specs,

time: 123 us -> 117 us (0.951)
  Pallas kernels: 122 us -> 116 us
    pallas_call x1, Pallas kernels: 116 us -> 112 us  [grads(): pl.pallas_call(kernel, out_shape=[jax.ShapeDtypeStruct((T, D), BF), jax.S...]
where the time goes in v3:
time: 117 us
  Pallas kernels  116 us (99%)
    pallas_call x1, Pallas kernels, grads(): pl.pallas_call(kernel, out_shape=[jax.ShapeDtypeStruct((T, D), BF), jax.S...  112 us
    pallas_call x1, Pallas kernels, body(): pl.pallas_call(hand_over, grid=(2,), out_shape=[jax.ShapeDtypeStruct(o.sh...  4.43 us

profile of v3, /device:TPU:32, one launch (start us, length us, event | category | flops | bytes accessed | tf_op | source)
XLA Modules:
  0.0 116.7 jit_solution(6948594671195136952)
XLA Ops:
  0.6 111.6 %swiglu_backward.1 = (bf16[128,512]{1,0:T(8,128)(2,1)}, f32[512,896]{1,0:T(8,128)}, f32[512,896]{1,0:T(8,128)}, f32[512,896]{1,0:T(8,128)}) custom-call(bf16[128,512]{1,0:T(8,128)(2,1)} %x_in.1, bf16[128,512]{1,0:T(8,128)(2,1)} %g_in.1, bf16[128,896]{1,0:T(8,128)(2,1)} %gate_in.1, bf16[128,896]{1,0:T(8,128)(2,1)} %up_in.1, bf16[512,896]{1,0:T(8,128)(2,1)} %wg_in.1, ...), custom_call_target="tpu_custom_call" | custom-call | flops 11274289152 | bytes 10485760 | tf_op jit(solution)/shard_map/swiglu_backward/pallas_call | solution.py:443
  112.3 4.4 %hand_over.1 = (bf16[128,512]{1,0:T(8,128)(2,1)}, f32[512,896]{1,0:T(8,128)}, f32[512,896]{1,0:T(8,128)}, f32[512,896]{1,0:T(8,128)}) custom-call(bf16[128,512]{1,0:T(8,128)(2,1)} %get-tuple-element.8.refs_0_, f32[512,896]{1,0:T(8,128)} %get-tuple-element.9.refs_1_, f32[512,896]{1,0:T(8,128)} %get-tuple-element.10.refs_2_, f32[512,896]{1,0:T(8,128)} %get-tuple-element.11.refs_3_), custom_call_target="tpu_custom_call" | custom-call | tf_op jit(solution)/shard_map/hand_over/pallas_call | solution.py:511

commit v4 on v3

--- a/solution.py
+++ b/solution.py
@@ -170,7 +170,7 @@
             for yy in range(4):
                 HF[n, 2 * yy : 2 * yy + 2] = part[:, yy]
                 HP[n, 2 * yy : 2 * yy + 2] = part[:, yy].astype(BF)
-            for d in (1, 3, 2):
+            for d in (2, 1, 3):
                 to = 2 * ((y + d) % 4)
                 send(HP.at[n, pl.ds(to, 2)], HR.at[n, pl.ds(2 * d - 2, 2)], xs.at[n, d], xr.at[n, d], at(dy=d))
 
@@ -183,11 +183,11 @@
                 t = HF[n, 4 * zl + yy] + HR[n, yy].astype(F32)
                 HF[n, 4 * zl + yy] = t
                 HP[n, 4 * zl + yy] = t.astype(BF)
-            for d in (1, 3, 2):
+            for d in (2, 1, 3):
                 to = 4 * zl + (y + d) % 4
                 send(HP.at[n, to], HR.at[n, 3 + d], xs.at[n, d], xr.at[n, d], at(dy=d))
         else:
-            for d in (1, 3, 2):
+            for d in (2, 1, 3):
                 arrived(HR.at[n, pl.ds(2 * d - 2, 2)], xr.at[n, d])
 
             def total(z):
@@ -208,7 +208,7 @@
                 arrived(HR.at[n, j - 1], xr.at[n, j])
                 t = t + HR[n, j - 1].astype(F32)
         elif ZSUM[n]:
-            for d in (1, 3, 2):
+            for d in (2, 1, 3):
                 arrived(HR.at[n, 3 + d], xr.at[n, d])
             t = HF[n, 4 * zl + y]
             for d in (1, 2, 3):
@@ -219,10 +219,10 @@
         HG[b + zl, y] = t.astype(BF)
         own = HG.at[b + zl, y]
         send(own, own, xs.at[n, 8], xr.at[n, 8], at(dzl=1))
-        for d in (1, 3, 2):
+        for d in (2, 1, 3):
             send(own, own, xs.at[n, 8 + d], xr.at[n, 8 + d], at(dy=d))
         if ZGATHER[n] == 2:
-            for d in (1, 3, 2):
+            for d in (2, 1, 3):
                 send(own, own, xs.at[n, 11 + d], xr.at[n, 11 + d], at(dzl=1, dy=d))
 
     def stage_d(n):
@@ -232,17 +232,17 @@
         if ZGATHER[n]:
             theirs = HG.at[b + 1 - zl, y]
             arrived(theirs, xr.at[n, 8])
-            for d in (1, 3, 2):
+            for d in (2, 1, 3):
                 send(theirs, theirs, xs.at[n, 11 + d], xr.at[n, 11 + d], at(dy=d))
         else:
-            for d in (1, 3, 2):
+            for d in (2, 1, 3):
                 theirs = HG.at[b + zl, (y + 4 - d) % 4]
                 arrived(theirs, xr.at[n, 8 + d])
                 send(theirs, theirs, xs.at[n, 11 + d], xr.at[n, 11 + d], at(dzl=1))
 
     def stage_e(n):
         b = base(n)
-        for d in (1, 3, 2):
+        for d in (2, 1, 3):
             yy = (y + 4 - d) % 4
             if ZGATHER[n]:
                 arrived(HG.at[b + zl, yy], xr.at[n, 8 + d])
@@ -307,7 +307,7 @@
 
     def sum_z2():
         t = IPO[2, zh // 2]
-        for e in (1, 3, 2):
+        for e in (2, 1, 3):
             arrived(IZ2.at[e - 1], rr.at[2, 4 + e])
             t = t + IZ2[e - 1].astype(F32)
         IXS[...] = t.astype(BF)
@@ -421,6 +421,8 @@
     weight_grad(1, XF, DG, gg_out)
     weight_grad(2, XF, DU, gu_out)
 
+    for cp in started:
+        cp.wait_send()
     t = IPO[0, zh // 2]
     for e in (1, 2, 3):
         arrived(IZR.at[e - 1], rr.at[2, e])
@@ -433,8 +435,6 @@
     outs.append(cp)
     for cp in outs:
         cp.wait()
-    for cp in started:
-        cp.wait_send()
 
 
 def grads(*args):

time: 117 us -> 116 us (level)
  no operation moved by 1% of the time
where the time goes in v4:
time: 116 us
  Pallas kernels  116 us (100%)
    pallas_call x1, Pallas kernels, grads(): pl.pallas_call(kernel, out_shape=[jax.ShapeDtypeStruct((T, D), BF), jax.S...  111 us
    pallas_call x1, Pallas kernels, body(): pl.pallas_call(hand_over, grid=(2,), out_shape=[jax.ShapeDtypeStruct(o.sh...  4.43 us

profile of v4, /device:TPU:32, one launch (start us, length us, event | category | flops | bytes accessed | tf_op | source)
XLA Modules:
  0.0 116.1 jit_solution(2361769816335338209)
XLA Ops:
  0.6 111.1 %swiglu_backward.1 = (bf16[128,512]{1,0:T(8,128)(2,1)}, f32[512,896]{1,0:T(8,128)}, f32[512,896]{1,0:T(8,128)}, f32[512,896]{1,0:T(8,128)}) custom-call(bf16[128,512]{1,0:T(8,128)(2,1)} %x_in.1, bf16[128,512]{1,0:T(8,128)(2,1)} %g_in.1, bf16[128,896]{1,0:T(8,128)(2,1)} %gate_in.1, bf16[128,896]{1,0:T(8,128)(2,1)} %up_in.1, bf16[512,896]{1,0:T(8,128)(2,1)} %wg_in.1, ...), custom_call_target="tpu_custom_call" | custom-call | flops 11274289152 | bytes 10485760 | tf_op jit(solution)/shard_map/swiglu_backward/pallas_call | solution.py:443
  111.7 4.4 %hand_over.1 = (bf16[128,512]{1,0:T(8,128)(2,1)}, f32[512,896]{1,0:T(8,128)}, f32[512,896]{1,0:T(8,128)}, f32[512,896]{1,0:T(8,128)}) custom-call(bf16[128,512]{1,0:T(8,128)(2,1)} %get-tuple-element.8.refs_0_, f32[512,896]{1,0:T(8,128)} %get-tuple-element.9.refs_1_, f32[512,896]{1,0:T(8,128)} %get-tuple-element.10.refs_2_, f32[512,896]{1,0:T(8,128)} %get-tuple-element.11.refs_3_), custom_call_target="tpu_custom_call" | custom-call | tf_op jit(solution)/shard_map/hand_over/pallas_call | solution.py:511
